TPU v7x, 32 devices: a whole 2x2x4 slice. The times are simulated.
32 devices in a mesh: ctx: 8 (over z, y), head: 4 (over x, core).
Axes of the slice: x: 2, y: 2, z: 4, core: 2. Of those that a mesh axis runs over, the one named last changes fastest.
Arguments:
- tokens: bfloat16 [4096, 1024], P(('ctx', 'head')), may hold values from -6 to 6
- conv_kernel: float32 [7, 1024], replicated, may hold values from -2.5 to 2.5
- w_qkv: bfloat16 [1024, 3072], replicated, may hold values from -0.1875 to 0.1875
- w_out: bfloat16 [1024, 1024], replicated, may hold values from -0.1875 to 0.1875
- lengths: int32 [4], replicated, may hold values from 1 to 2048, 4096 in all
- cotangent: bfloat16 [4096, 1024], P(('ctx', 'head')), may hold values from -6 to 6
Outputs:
- attended: bfloat16 [4096, 1024], P(('ctx', 'head'))
- input_grad: bfloat16 [4096, 1024], P(('ctx', 'head'))
Inputs may be any that keep to these rules, and one draw needn't show every extreme that they name: `lengths`: they sum to 4096; the longest recording has exactly 2048 tokens.
All inputs are finite; a program needn't handle non-finite values.
Results may differ from a plain program's by a relative error of at most 0.017.
The roundings to bfloat16 on the way count: a program that leaves them out, or rounds other values in their place, can miss the bound.
Values may be sent and summed in bfloat16 or wider, within the bound.
No kernel may reach another device: no remote copies, remote signals or barrier semaphores. Data moves between devices by JAX's collectives and lax.ppermute only.
A program may use at most 128 MiB of HBM per device.

v0:
```python
import functools
import math

import jax
import jax.numpy as jnp
from jax import lax
from jax.experimental import pallas as pl
from jax.experimental.pallas import tpu as pltpu
from jax.sharding import PartitionSpec as P

HD = 64
KS = 7
HALF = KS // 2
MAXLEN = 2048
AXES = ("ctx", "head")
LANES = 128
EDGE = 16
PER_STEP = 2
VMEM_ALL = 60 * 1024 * 1024
VMEM_MOST = 44 * 1024 * 1024
VMEM_SOME = 24 * 1024 * 1024
VMEM_FEW = 16 * 1024 * 1024
F32 = jnp.float32
BF16 = jnp.bfloat16


def params(limit):
    return pltpu.CompilerParams(vmem_limit_bytes=limit)


def record_span(positions, lengths_ref):
    start = jnp.zeros_like(positions)
    stop = jnp.full_like(positions, jnp.iinfo(jnp.int32).max)
    end = jnp.int32(0)
    for i in range(lengths_ref.shape[0]):
        end = end + lengths_ref[i]
        past = end <= positions
        start = jnp.where(past, end, start)
        stop = jnp.where(past, stop, jnp.minimum(stop, end))
    return start, stop


def low_lanes(shape):
    return lax.broadcasted_iota(jnp.int32, shape, len(shape) - 1) % LANES < HD


def swap_halves(x):
    return pltpu.roll(x, HD, x.ndim - 1)


def zip_low(x, y):
    return jnp.where(low_lanes(x.shape), x, swap_halves(y))


def zip_high(x, y):
    return jnp.where(low_lanes(x.shape), swap_halves(x), y)


def conv_rows(padded_ref, cols, kernel_ref, lengths_ref, first_row, rows, flip):
    pos = first_row + lax.broadcasted_iota(jnp.int32, (rows, LANES), 0)
    start, stop = record_span(pos, lengths_ref)
    masks = []
    for t in range(KS):
        at = pos + (t - HALF)
        masks.append((at >= start) & (at < stop))
    pieces = []
    for c in cols:
        lanes = pl.ds(c * LANES, LANES)
        total = padded_ref[pl.ds(8, rows), lanes]
        for t in range(KS):
            tap = kernel_ref[KS - 1 - t if flip else t, lanes]
            shifted = padded_ref[pl.ds(8 - HALF + t, rows), lanes]
            total = total + jnp.where(masks[t], shifted, 0.0) * tap[None, :]
        pieces.append(total)
    return jnp.concatenate(pieces, axis=1)


def front_kernel(
    lengths_ref, where_ref, before_ref, x_ref, after_ref, taps_ref, w_ref, cot_ref, wo_ref,
    out_ref, padded, projected, d_rows,
):
    rows, blk = x_ref.shape
    step = pl.program_id(0)
    steps = pl.num_programs(0)
    padded[pl.ds(0, 8), :] = before_ref[...].astype(F32)[EDGE - 8 :]
    padded[pl.ds(8, rows), :] = x_ref[...].astype(F32)
    padded[pl.ds(8 + rows, 8), :] = after_ref[...].astype(F32)[:8]
    mixed = conv_rows(
        padded, range(blk // LANES), taps_ref, lengths_ref, where_ref[0], rows, False
    ).astype(BF16)
    d_rows[step] = lax.dot_general(
        cot_ref[...], wo_ref[...], (((1,), (1,)), ((), ())), preferred_element_type=F32
    )
    part = jnp.dot(mixed, w_ref[...], preferred_element_type=F32)

    @pl.when(step == 0)
    def _():
        projected[...] = part

    @pl.when(step > 0)
    def _():
        projected[...] += part

    @pl.when(step == steps - 1)
    def _():
        width = projected.shape[1] // 3
        per = blk // LANES
        for pair in range(width // LANES):
            q, k, v = (projected[:, pl.ds(i * width + pair * LANES, LANES)] for i in range(3))
            d = d_rows[pair // per, :, pl.ds(pair % per * LANES, LANES)]
            out_ref[2 * pair] = jnp.concatenate([zip_low(k, v), zip_low(q, d)]).astype(BF16)
            out_ref[2 * pair + 1] = jnp.concatenate([zip_high(k, v), zip_high(q, d)]).astype(BF16)


def front_call(lengths, where, before, x, after, taps, w_qkv, cotangent, w_out):
    rows, width = x.shape
    heads = width // HD
    blk = 256
    smem = pl.BlockSpec(memory_space=pltpu.SMEM)
    columns = lambda a: pl.BlockSpec((a.shape[0], blk), lambda i: (0, i))
    return pl.pallas_call(
        front_kernel,
        grid=(width // blk,),
        in_specs=[
            smem, smem, columns(before), columns(x), columns(after), columns(taps),
            pl.BlockSpec((blk, 3 * width), lambda i: (i, 0)),
            pl.BlockSpec((rows, width), lambda i: (0, 0)),
            pl.BlockSpec((blk, width), lambda i: (i, 0)),
        ],
        out_specs=pl.BlockSpec((heads, 2 * rows, LANES), lambda i: (0, 0, 0)),
        out_shape=jax.ShapeDtypeStruct((heads, 2 * rows, LANES), BF16),
        scratch_shapes=[
            pltpu.VMEM((rows + 16, blk), F32),
            pltpu.VMEM((rows, 3 * width), F32),
            pltpu.VMEM((width // blk, rows, blk), F32),
        ],
        compiler_params=params(VMEM_ALL),
        cost_estimate=pl.CostEstimate(
            flops=8 * rows * width * width, bytes_accessed=8 * width * width, transcendentals=0
        ),
        name="front",
    )(lengths, where, before, x, after, taps, w_qkv, cotangent, w_out)


def attention_kernel(
    pre, place, lengths_ref, where_ref, kv_mine, kv_other, qd_ref,
    cq_ref, dkv_mine, edge_mine, send_ref,
    visit_q, visit_k, keys_ref, turned_ref, qd_cat_ref, d_turned_ref, span_ref, e_ref,
    total_ref, context_ref, row_ref, d_query_ref, acc_ref, cq_full,
):
    slots = qd_ref.shape[0]
    key_slots, rows, _ = kv_mine.shape
    tile = 2 * rows
    tiles, groups = key_slots // 2, slots // 2
    base, parity = where_ref[1], where_ref[2]
    origin = base - pre * tile
    unit = HD**-0.5
    to_exp2 = unit * math.log2(math.e)

    lane = lax.broadcasted_iota(jnp.int32, (1, tile), 1)
    lane_pos = (lane // rows) * tile + lane % rows
    sub = lax.broadcasted_iota(jnp.int32, (2 * tile, 1), 0)
    side = jnp.where(sub < tile, parity, 1 - parity)
    sub_pos = (sub // rows % 2) * tile + sub % rows + side * rows

    count = jnp.int32(0)
    for u in range(groups):
        first = base + u * (2 * tile) + parity * rows
        begin, end = jnp.int32(0), jnp.int32(0)
        for i in range(lengths_ref.shape[0]):
            end = end + lengths_ref[i]
            begin = jnp.where(end <= first, end, begin)
        t_first = jnp.maximum(begin - origin, 0) // (2 * tile)

        def note(t, count, u=u):
            visit_q[count] = u
            visit_k[count] = t
            return count + 1

        count = lax.fori_loop(t_first, u + pre // 2 + 1, note, count)
    visit_q[count] = groups
    visit_k[count] = tiles

    for t in range(tiles):
        for half, source in enumerate((kv_mine, kv_other)):
            block = jnp.concatenate([source[place(2 * t + i, pre)] for i in range(2)])
            keys_ref[t, pl.ds(half * tile, tile)] = block
            turned_ref[t, :, pl.ds(half * tile, tile)] = block.T
    keys_ref[tiles] = jnp.zeros_like(keys_ref[tiles])
    turned_ref[tiles] = jnp.zeros_like(turned_ref[tiles])
    acc_ref[...] = jnp.zeros_like(acc_ref)
    total_ref[...] = jnp.zeros_like(total_ref)
    context_ref[...] = jnp.zeros_like(context_ref)
    d_query_ref[...] = jnp.zeros_like(d_query_ref)
    for u in range(groups):
        qd = jnp.concatenate(
            [qd_ref[place(2 * u + i, 0), pl.ds(rows, rows)] for i in range(2)]
        ).astype(F32)
        low = low_lanes(qd.shape)
        qd_cat_ref[u, pl.ds(0, tile)] = jnp.where(low, qd, 0.0).astype(BF16)
        qd_cat_ref[u, pl.ds(tile, tile)] = jnp.where(low, 0.0, qd).astype(BF16)
        d_turned_ref[u] = qd.T[HD:]
        q_pos = base + u * (2 * tile) + parity * rows + lane_pos
        q_start, _ = record_span(q_pos, lengths_ref)
        span_ref[u, pl.ds(0, 1)] = q_start
        span_ref[u, pl.ds(1, 1)] = q_pos
    qd_cat_ref[groups] = jnp.zeros_like(qd_cat_ref[groups])
    span_ref[groups] = jnp.zeros_like(span_ref[groups])
    row_ref[groups] = jnp.zeros_like(row_ref[groups])

    def forward(i):
        u, t = visit_q[i], visit_k[i]
        scores = lax.dot_general(
            keys_ref[t], qd_cat_ref[u, pl.ds(0, tile)], (((1,), (1,)), ((), ())),
            preferred_element_type=F32,
        )
        k_pos = origin + t * (2 * tile) + sub_pos
        span = span_ref[u]
        allowed = (k_pos >= span[0:1]) & (k_pos <= span[1:2])
        e = jnp.where(allowed, jnp.exp2(scores * to_exp2), 0.0)
        e_ref[i] = e
        context = jnp.dot(turned_ref[t, HD:], e.astype(BF16), preferred_element_type=F32)
        return u, jnp.sum(e.reshape(2 * tile // 8, 8, tile), axis=0), context

    def forward_some(j, carry):
        for u, total, context in [forward(PER_STEP * j + i) for i in range(PER_STEP)]:
            total_ref[u] += total
            context_ref[u] += context
        return carry

    steps = (count + PER_STEP - 1) // PER_STEP
    lax.fori_loop(0, steps, forward_some, 0)
    for u in range(groups):
        inverse = 1.0 / jnp.sum(total_ref[u], axis=0, keepdims=True)
        context = (context_ref[u] * inverse).astype(BF16).astype(F32)
        context_ref[u] = context
        row_ref[u, pl.ds(0, 1)] = inverse
        row_ref[u, pl.ds(1, 1)] = jnp.sum(d_turned_ref[u] * context, axis=0, keepdims=True)

    def backward(i):
        u, t = visit_q[i], visit_k[i]
        row = row_ref[u]
        probs = e_ref[i] * row[0:1]
        d_probs = lax.dot_general(
            keys_ref[t], qd_cat_ref[u, pl.ds(tile, tile)], (((1,), (1,)), ((), ())),
            preferred_element_type=F32,
        )
        d_scores = (probs * (d_probs - row[1:2])).astype(BF16)
        both = jnp.concatenate([d_scores, probs.astype(BF16)], axis=1)
        d_keys = jnp.dot(both, qd_cat_ref[u], preferred_element_type=F32)
        d_queries = jnp.dot(turned_ref[t, :HD], d_scores, preferred_element_type=F32)
        return u, t, d_keys, d_queries

    def backward_some(j, carry):
        for u, t, d_keys, d_queries in [backward(PER_STEP * j + i) for i in range(PER_STEP)]:
            acc_ref[t] += d_keys
            d_query_ref[u] += d_queries
        return carry

    lax.fori_loop(0, steps, backward_some, 0)
    for u in range(groups):
        packed = jnp.concatenate([context_ref[u], d_query_ref[u] * unit], axis=0).T
        for i in range(2):
            part = packed[i * rows : (i + 1) * rows]
            cq_full[2 * u + i] = part
            cq_ref[2 * u + i] = part.astype(BF16)
    scale = jnp.where(low_lanes((1, LANES)), unit, 1.0)
    head = lax.broadcasted_iota(jnp.int32, (8, LANES), 0) < 4

    def end_rows(half, slot, first):
        slot = pre + jnp.clip(slot, 0, slots - 1)
        at = half * tile + slot % 2 * rows + first
        return acc_ref[slot // 2, pl.ds(pl.multiple_of(at, 8), 8)] * scale

    for s in range(key_slots):
        part = pl.ds(s % 2 * rows, rows)
        dkv_mine[s] = acc_ref[s // 2, part] * scale
        part = pl.ds(tile + s % 2 * rows, rows)
        send_ref[s, pl.ds(0, rows)] = (acc_ref[s // 2, part] * scale).astype(BF16)
        if s < pre:
            send_ref[s, pl.ds(rows, 16)] = jnp.zeros((16, LANES), BF16)
    for s in range(slots):
        edge_mine[s] = jnp.where(
            head, end_rows(1, s + parity, 0), end_rows(1, s - 1 + parity, rows - 8)
        )
        past, later = s - parity, s + 1 - parity
        d_edge = jnp.where(head, end_rows(0, later, 0), end_rows(0, past, rows - 8))
        q_edge = jnp.where(
            head,
            cq_full[jnp.clip(later, 0, slots - 1), pl.ds(0, 8)],
            cq_full[jnp.clip(past, 0, slots - 1), pl.ds(rows - 8, 8)],
        )
        send_ref[pre + s, pl.ds(rows, 16)] = jnp.concatenate([d_edge, q_edge]).astype(BF16)


def attention_call(lengths, where, kv_mine, kv_other, qd, pre):
    slots = qd.shape[0]
    key_slots, rows, _ = kv_mine.shape
    tile = 2 * rows
    tiles, groups = key_slots // 2, slots // 2
    reach = MAXLEN // (2 * tile) + 1
    place = lambda s, ordered: s if ordered else bit_reversed(s, slots)
    visits = sum(min(u + pre // 2 + 1, reach) for u in range(groups)) + PER_STEP - 1
    smem = pl.BlockSpec(memory_space=pltpu.SMEM)
    vmem = pl.BlockSpec(memory_space=pltpu.VMEM)
    return pl.pallas_call(
        functools.partial(attention_kernel, pre, place),
        in_specs=[smem, smem, vmem, vmem, vmem],
        out_specs=[vmem, vmem, vmem, vmem],
        out_shape=[
            jax.ShapeDtypeStruct((slots, rows, LANES), BF16),
            jax.ShapeDtypeStruct((key_slots, rows, LANES), F32),
            jax.ShapeDtypeStruct((slots, 8, LANES), F32),
            jax.ShapeDtypeStruct((key_slots, rows + 16, LANES), BF16),
        ],
        scratch_shapes=[
            pltpu.SMEM((visits + 1,), jnp.int32),
            pltpu.SMEM((visits + 1,), jnp.int32),
            pltpu.VMEM((tiles + 1, 2 * tile, LANES), BF16),
            pltpu.VMEM((tiles + 1, LANES, 2 * tile), BF16),
            pltpu.VMEM((groups + 1, 2 * tile, LANES), BF16),
            pltpu.VMEM((groups, HD, tile), F32),
            pltpu.VMEM((groups + 1, 8, tile), jnp.int32),
            pltpu.VMEM((visits, 2 * tile, tile), F32),
            pltpu.VMEM((groups + 1, 8, tile), F32),
            pltpu.VMEM((groups + 1, HD, tile), F32),
            pltpu.VMEM((groups + 1, 8, tile), F32),
            pltpu.VMEM((groups + 1, HD, tile), F32),
            pltpu.VMEM((tiles + 1, 2 * tile, LANES), F32),
            pltpu.VMEM((slots, rows, LANES), F32),
        ],
        compiler_params=params(VMEM_MOST),
        cost_estimate=pl.CostEstimate(
            flops=10 * slots * rows * MAXLEN * LANES,
            bytes_accessed=20 * slots * rows * LANES,
            transcendentals=slots * rows * MAXLEN,
        ),
        name="attention",
    )(lengths, where, kv_mine, kv_other, qd)


def combine_kernel(cq_ref, mine_ref, edge_ref, got_ref, out_ref):
    slots, rows, _ = cq_ref.shape
    for s in range(slots):
        at = bit_reversed(s, slots)
        out_ref[at, pl.ds(0, rows)] = cq_ref[s]
        got = got_ref[s].astype(F32)
        out_ref[at, pl.ds(rows, rows)] = (mine_ref[s] + got[:rows]).astype(BF16)
        edges = [edge_ref[s] + got[rows : rows + 8], got[rows + 8 :]]
        out_ref[at, pl.ds(2 * rows, 16)] = jnp.concatenate(edges).astype(BF16)


def combine_call(cq, mine, edge, got):
    slots, rows, _ = cq.shape
    vmem = pl.BlockSpec(memory_space=pltpu.VMEM)
    return pl.pallas_call(
        combine_kernel,
        in_specs=[vmem] * 4,
        out_specs=vmem,
        out_shape=jax.ShapeDtypeStruct((slots, 2 * rows + 16, LANES), BF16),
        compiler_params=params(VMEM_SOME),
        name="combine",
    )(cq, mine, edge, got)


def combine_windows(cq, mine, got, pre, side, window, devices):
    slots, rows, _ = cq.shape
    dkv = mine + got[:, :rows].astype(F32)
    back = [(i + window, i) for i in range(devices - window)]
    earlier = lax.ppermute(dkv[:pre].astype(BF16), AXES, back).astype(F32)
    dkv = dkv[pre:].at[slots - pre :].add(earlier).astype(BF16)
    both = jnp.concatenate([cq, dkv], axis=2)
    tails, heads = both[:, rows - 8 :], both[:, :8]
    swapped = [(i, i ^ 1) for i in range(devices)]
    tails_other = lax.ppermute(tails, AXES, swapped)
    heads_other = lax.ppermute(heads, AXES, swapped)
    last = [(i, i + window - 1) for i in range(1, devices - window, 2)]
    tail_past = lax.ppermute(tails[-1:], AXES, last)
    head_next = lax.ppermute(heads[:1], AXES, [(j, i) for i, j in last])
    before = jnp.where(
        side == 0, jnp.concatenate([tail_past, tails_other[:-1]]), tails_other
    )
    after = jnp.where(side == 0, heads_other, jnp.concatenate([heads_other[1:], head_next]))
    edge = jnp.where(jnp.arange(8)[None, :, None] < 4, after, before)
    grads = jnp.concatenate([cq, dkv, edge[..., LANES:], edge[..., :LANES]], axis=1)
    return jnp.stack([grads[bit_reversed(s, slots)] for s in range(slots)])


def back_kernel(
    lengths_ref, where_ref, r_ref, taps_ref, w_ref, wo_ref,
    attended_ref, grad_ref, context, grads, padded,
):
    heads = r_ref.shape[0]
    rows = context.shape[0]
    width = heads * HD
    blk = grad_ref.shape[1]

    @pl.when(pl.program_id(0) == 0)
    def _():
        for pair in range(heads // 2):
            lanes = pl.ds(pair * LANES, LANES)
            x, y = (r_ref[2 * pair + i].astype(F32) for i in range(2))
            main, dkv, edge_dkv, edge_cq = (
                (slice(0, rows)), slice(rows, 2 * rows),
                slice(2 * rows, 2 * rows + 8), slice(2 * rows + 8, 2 * rows + 16),
            )
            context[:, lanes] = zip_low(x[main], y[main]).astype(BF16)
            pad = jnp.zeros((8, LANES), F32)

            def gather(mix, part, edge):
                return jnp.concatenate(
                    [mix(x[part], y[part]), mix(x[edge], y[edge]), pad]
                ).astype(BF16)

            grads[:, lanes] = gather(zip_high, main, edge_cq)
            grads[:, pl.ds(width + pair * LANES, LANES)] = gather(zip_low, dkv, edge_dkv)
            grads[:, pl.ds(2 * width + pair * LANES, LANES)] = gather(zip_high, dkv, edge_dkv)

    attended_ref[...] = jnp.dot(context[...], wo_ref[...], preferred_element_type=F32).astype(BF16)
    mixed = lax.dot_general(
        grads[...], w_ref[...], (((1,), (1,)), ((), ())), preferred_element_type=F32
    ).astype(BF16).astype(F32)
    edge = mixed[rows : rows + 8]
    padded[pl.ds(0, 8), :] = edge
    padded[pl.ds(8, rows), :] = mixed[:rows]
    padded[pl.ds(8 + rows, 8), :] = edge
    grad_ref[...] = conv_rows(
        padded, range(blk // LANES), taps_ref, lengths_ref, where_ref[0], rows, True
    ).astype(BF16)


def back_call(lengths, where, r, taps, w_qkv, w_out):
    heads = r.shape[0]
    rows = (r.shape[1] - 16) // 2
    width = heads * HD
    blk = 256
    smem = pl.BlockSpec(memory_space=pltpu.SMEM)
    out = pl.BlockSpec((rows, blk), lambda i: (0, i))
    shape = jax.ShapeDtypeStruct((rows, width), BF16)
    return pl.pallas_call(
        back_kernel,
        grid=(width // blk,),
        in_specs=[
            smem, smem,
            pl.BlockSpec(r.shape, lambda i: (0, 0, 0)),
            pl.BlockSpec((KS, blk), lambda i: (0, i)),
            pl.BlockSpec((blk, 3 * width), lambda i: (i, 0)),
            pl.BlockSpec((width, blk), lambda i: (0, i)),
        ],
        out_specs=[out, out],
        out_shape=[shape, shape],
        scratch_shapes=[
            pltpu.VMEM((rows, width), BF16),
            pltpu.VMEM((rows + 16, 3 * width), BF16),
            pltpu.VMEM((rows + 16, blk), F32),
        ],
        compiler_params=params(VMEM_FEW),
        cost_estimate=pl.CostEstimate(
            flops=8 * rows * width * width, bytes_accessed=8 * width * width, transcendentals=0
        ),
        name="back",
    )(lengths, where, r, taps, w_qkv, w_out)


def bit_reversed(i, count):
    bits = count.bit_length() - 1
    if count != 1 << bits:
        return i
    return sum((i >> b & 1) << (bits - 1 - b) for b in range(bits))


def on_device(tokens, conv_kernel, w_qkv, w_out, lengths, cotangent):
    rows, width = tokens.shape
    heads = width // HD
    devices = lax.axis_size(AXES)
    window = 2 * heads
    windows = devices // window
    pre = MAXLEN // (2 * rows) if windows > 1 else 0
    me = lax.axis_index(AXES)
    where = jnp.stack([me * rows, me // window * (window * rows), me % 2]).astype(jnp.int32)
    same_side = [
        [w * window + 2 * bit_reversed(c, heads) + side for c in range(heads)]
        for w in range(windows)
        for side in range(2)
    ]
    swapped = [(i, i ^ 1) for i in range(devices)]
    up = [(i, i + 1) for i in range(devices - 1)]
    down = [(i + 1, i) for i in range(devices - 1)]

    def exchange(x):
        return lax.all_to_all(
            x, AXES, split_axis=0, concat_axis=0, axis_index_groups=same_side, tiled=True
        )

    before = lax.ppermute(tokens[rows - EDGE :], AXES, up)
    after = lax.ppermute(tokens[:EDGE], AXES, down)
    sent = front_call(lengths, where, before, tokens, after, conv_kernel, w_qkv, cotangent, w_out)
    qd = exchange(sent)
    kv_mine = qd[:, :rows]
    if pre:
        shift = [(i, i + window) for i in range(devices - window)]
        kv_mine = jnp.stack([kv_mine[bit_reversed(s, heads)] for s in range(heads)])
        kv_mine = jnp.concatenate([lax.ppermute(kv_mine[heads - pre :], AXES, shift), kv_mine])
    kv_other = lax.ppermute(kv_mine, AXES, swapped)
    cq, mine, edge, send = attention_call(lengths, where, kv_mine, kv_other, qd, pre)
    got = lax.ppermute(send, AXES, swapped)
    if pre:
        grads = combine_windows(cq, mine, got, pre, me % 2, window, devices)
    else:
        grads = combine_call(cq, mine, edge, got)
    return back_call(lengths, where, exchange(grads), conv_kernel, w_qkv, w_out)


def solution(mesh):
    placed = (P(AXES, None), P(), P(), P(), P(), P(AXES, None))
    return jax.shard_map(
        on_device,
        mesh=mesh,
        in_specs=placed,
        out_specs=(P(AXES, None), P(AXES, None)),
        check_vma=False,
    )
```

profile of v0, /device:TPU:0, one launch (start us, length us, event | category | flops | bytes accessed | tf_op | source)
XLA Modules:
  0.0 114.0 jit_solution(5404247125474871259)
XLA Ops:
  0.6 0.8 fusion
  1.4 1.3 %collective-permute-start.1 = (bf16[16,1024]{1,0:T(8,128)(2,1)S(1)}, bf16[16,1024]{1,0:T(8,128)(2,1)S(1)}, u32[]{:S(2)}, u32[]{:S(2)}) collective-permute-start(bf16[16,1024]{1,0:T(8,128)(2,1)S(1)} %get-tuple-element.10), channel_id=1, source_target_pairs={{1,0},{2,1},{3,2},{4,3},{5,4},{6,5},{7,6},{8,7},{9,8},{10,9},{11,1... | collective-permute-start | bytes 98312 | tf_op jit(solution)/shard_map/ppermute | solution.py:496
  2.7 3.0 %collective-permute-start = (bf16[16,1024]{1,0:T(8,128)(2,1)S(1)}, bf16[16,1024]{1,0:T(8,128)(2,1)S(1)}, u32[]{:S(2)}, u32[]{:S(2)}) collective-permute-start(bf16[16,1024]{1,0:T(8,128)(2,1)S(1)} %get-tuple-element.11), channel_id=1, source_target_pairs={{0,1},{1,2},{2,3},{3,4},{4,5},{5,6},{6,7},{7,8},{8,9},{9,10},{10,1... | collective-permute-start | bytes 98312 | tf_op jit(solution)/shard_map/ppermute | solution.py:495
  5.8 0.6 pad_add_fusion.where_ref
  6.4 0.0 collective-permute-done.1.after_ref
  6.4 0.2 collective-permute-done.before_ref
  6.6 0.4 copy-done.4
  7.0 0.6 copy-done.5
  7.6 7.7 %front.1 = bf16[16,256,128]{2,1,0:T(8,128)(2,1)} custom-call(s32[4]{0:T(128)} %lengths_ref.5, s32[3]{0:T(128)} %pad_add_fusion.where_ref, bf16[16,1024]{1,0:T(8,128)(2,1)} %copy-done.5, bf16[128,1024]{1,0:T(8,128)(2,1)} %x_ref.1, bf16[16,1024]{1,0:T(8,128)(2,1)} %copy-done.4, f32[7,1024]{1,0:T(8,128)} %taps_ref.3, bf16[1024,3072]{1,0:T(8,128)(2,1)} %w_ref.3, ...), custom_call_target="tpu_custom_call" | custom-call | flops 1073741824 | bytes 8388608 | tf_op jit(solution)/shard_map/front/pallas_call | solution.py:121
  15.3 36.2 %all_to_all.10.qd_ref = bf16[16,256,128]{2,1,0:T(8,128)(2,1)S(1)} all-to-all(bf16[16,256,128]{2,1,0:T(8,128)(2,1)} %front.1), channel_id=1, replica_groups={{0,16,8,24,4,20,12,28,2,18,10,26,6,22,14,30},{1,17,9,25,5,21,13,29,3,19..., dimensions={0} | all-to-all | bytes 2097152 | tf_op jit(solution)/shard_map/all_to_all | solution.py:491
  51.6 0.0 slice-start.1
  51.6 0.1 collective-permute-start.2
  51.6 1.9 %collective-permute-done.2.kv_other = bf16[16,128,128]{2,1,0:T(8,128)(2,1)S(1)} collective-permute-done((bf16[16,128,128]{2,1,0:T(8,128)(2,1)S(1)}, bf16[16,128,128]{2,1,0:T(8,128)(2,1)S(1)}, u32[]{:S(2)}, u32[]{:S(2)}) %collective-permute-start.2) | collective-permute-done | bytes 524320 | tf_op jit(solution)/shard_map/ppermute | solution.py:504
  53.5 0.0 copy-done.2
  53.5 0.0 copy-done.3
  53.5 19.2 %attention.1 = (bf16[16,128,128]{2,1,0:T(8,128)(2,1)S(1)}, f32[16,128,128]{2,1,0:T(8,128)S(1)}, f32[16,8,128]{2,1,0:T(8,128)S(1)}, bf16[16,144,128]{2,1,0:T(8,128)(2,1)S(1)}) custom-call(s32[4]{0:T(128)S(1)} %copy-done.3, s32[3]{0:T(128)S(1)} %copy-done.2, bf16[16,128,128]{2,1,0:T(8,128)(2,1)S(1)} %slice.12.kv_mine, ...), custom_call_target="tpu_custom_call" | custom-call | flops 5368709120 | bytes 5242880 | tf_op jit(solution)/shard_map/attention/pallas_call | solution.py:306
  72.7 0.1 collective-permute-start.3
  72.8 2.0 %collective-permute-done.3.got_ref = bf16[16,144,128]{2,1,0:T(8,128)(2,1)S(1)} collective-permute-done((bf16[16,144,128]{2,1,0:T(8,128)(2,1)S(1)}, bf16[16,144,128]{2,1,0:T(8,128)(2,1)S(1)}, u32[]{:S(2)}, u32[]{:S(2)}) %collective-permute-start.3) | collective-permute-done | bytes 589856 | tf_op jit(solution)/shard_map/ppermute | solution.py:506
  74.8 0.2 combine.1
  74.9 32.9 %all_to_all.11.r_ref = bf16[16,272,128]{2,1,0:T(8,128)(2,1)S(1)} all-to-all(bf16[16,272,128]{2,1,0:T(8,128)(2,1)S(1)} %combine.1), channel_id=1, replica_groups={{0,16,8,24,4,20,12,28,2,18,10,26,6,22,14,30},{1,17,9,25,5,21,13,29,3,19..., dimensions={0} | all-to-all | bytes 2228224 | tf_op jit(solution)/shard_map/all_to_all | solution.py:491
  107.8 0.0 slice-done
  107.8 0.0 slice-done.1
  107.8 0.0 copy-done
  107.9 6.1 %back.1 = (bf16[128,1024]{1,0:T(8,128)(2,1)}, bf16[128,1024]{1,0:T(8,128)(2,1)}) custom-call(s32[4]{0:T(128)S(1)} %copy-done.3, s32[3]{0:T(128)S(1)} %copy-done.2, bf16[16,272,128]{2,1,0:T(8,128)(2,1)S(1)} %all_to_all.11.r_ref, f32[7,1024]{1,0:T(8,128)S(1)} %copy-done.1, bf16[1024,3072]{1,0:T(8,128)(2,1)S(1)} %bitcast.4, bf16[1024,1024]{1,0:T(8,128)(2,1)S(1)} %copy-done), custom_call_target="tpu_custom_call" | custom-call | flops 1073741824 | bytes 8388608 | tf_op jit(solution)/shard_map/back/pallas_call | solution.py:440
  (10 shorter events, 0.1 us)
Async XLA Ops:
  1.4 5.0 %collective-permute-start.1 = (bf16[16,1024]{1,0:T(8,128)(2,1)S(1)}, bf16[16,1024]{1,0:T(8,128)(2,1)S(1)}, u32[]{:S(2)}, u32[]{:S(2)}) collective-permute-start(bf16[16,1024]{1,0:T(8,128)(2,1)S(1)} %get-tuple-element.10), channel_id=1, source_target_pairs={{1,0},{2,1},{3,2},{4,3},{5,4},{6,5},{7,6},{8,7},{9,8},{10,9},{11,1... | collective-permute-start | bytes 98312 | tf_op jit(solution)/shard_map/ppermute | solution.py:496
  2.7 3.9 %collective-permute-start = (bf16[16,1024]{1,0:T(8,128)(2,1)S(1)}, bf16[16,1024]{1,0:T(8,128)(2,1)S(1)}, u32[]{:S(2)}, u32[]{:S(2)}) collective-permute-start(bf16[16,1024]{1,0:T(8,128)(2,1)S(1)} %get-tuple-element.11), channel_id=1, source_target_pairs={{0,1},{1,2},{2,3},{3,4},{4,5},{5,6},{6,7},{7,8},{8,9},{9,10},{10,1... | collective-permute-start | bytes 98312 | tf_op jit(solution)/shard_map/ppermute | solution.py:495
  6.4 0.6 copy-start.4
  7.0 0.6 copy-start.5
  15.3 38.2 %copy-start.2 = (s32[3]{0:T(128)S(1)}, s32[3]{0:T(128)}, u32[]{:S(2)}) copy-start(s32[3]{0:T(128)} %pad_add_fusion.where_ref) | copy-start | bytes 40
  15.3 38.2 %copy-start.3 = (s32[4]{0:T(128)S(1)}, s32[4]{0:T(128)}, u32[]{:S(2)}) copy-start(s32[4]{0:T(128)} %lengths_ref.5) | copy-start | bytes 52
  51.5 56.3 %slice-start = ((s8[6291456]{0:T(1024)(128)(4,1)}), s8[4194304]{0:T(1024)(128)(4,1)S(1)}, s32[]{:S(2)}) async-start(s8[6291456]{0:T(1024)(128)(4,1)} %bitcast.3), calls=%async_computation.2 | async-start | bytes 8388608
  51.6 56.3 %slice-start.1 = ((s8[6291456]{0:T(1024)(128)(4,1)}), s8[2097152]{0:T(1024)(128)(4,1)S(1)}, s32[]{:S(2)}) async-start(s8[6291456]{0:T(1024)(128)(4,1)} %bitcast.3), calls=%async_computation.3 | async-start | bytes 4194304
  51.6 2.0 %collective-permute-start.2 = (bf16[16,128,128]{2,1,0:T(8,128)(2,1)S(1)}, bf16[16,128,128]{2,1,0:T(8,128)(2,1)S(1)}, u32[]{:S(2)}, u32[]{:S(2)}) collective-permute-start(bf16[16,128,128]{2,1,0:T(8,128)(2,1)S(1)} %slice.12.kv_mine), channel_id=1, source_target_pairs={{0,1},{1,0},{2,3},{3,2},{4,5},{5,4},{6,7},{7,6},{8,9},{9,8},{10,11... | collective-permute-start | bytes 1572872 | tf_op jit(solution)/shard_map/ppermute | solution.py:504
  72.7 2.1 %collective-permute-start.3 = (bf16[16,144,128]{2,1,0:T(8,128)(2,1)S(1)}, bf16[16,144,128]{2,1,0:T(8,128)(2,1)S(1)}, u32[]{:S(2)}, u32[]{:S(2)}) collective-permute-start(bf16[16,144,128]{2,1,0:T(8,128)(2,1)S(1)} %get-tuple-element.9), channel_id=1, source_target_pairs={{0,1},{1,0},{2,3},{3,2},{4,5},{5,4},{6,7},{7,6},{8,9},{9,8},{10,11... | collective-permute-start | bytes 1769480 | tf_op jit(solution)/shard_map/ppermute | solution.py:506
  74.8 33.1 %copy-start = (bf16[1024,1024]{1,0:T(8,128)(2,1)S(1)}, bf16[1024,1024]{1,0:T(8,128)(2,1)}, u32[]{:S(2)}) copy-start(bf16[1024,1024]{1,0:T(8,128)(2,1)} %wo_ref.3) | copy-start | bytes 6291460
  74.8 33.1 %copy-start.1 = (f32[7,1024]{1,0:T(8,128)S(1)}, f32[7,1024]{1,0:T(8,128)}, u32[]{:S(2)}) copy-start(f32[7,1024]{1,0:T(8,128)} %taps_ref.3) | copy-start | bytes 86020
where the time goes:
time: 113 us; the launch traced here: 114 us
  blocking collectives  69.1 us (61%)
  Pallas kernels  33.1 us (29%)
  starting transfers between devices  4.45 us (4%)
  waiting for transfers between devices  4.08 us (4%)
  local copies, waits for them, and re-layouts  1.89 us (2%)
    all_to_all x2, blocking collectives, exchange(): lax.all_to_all(x, AXES, split_axis=0, concat_axis=0, axis_index_groups=sa...  69.1 us
    pallas_call x1, Pallas kernels, attention_call(): pl.pallas_call(functools.partial(attention_kernel, pre, place), in_specs=...  19.2 us
    pallas_call x1, Pallas kernels, front_call(): pl.pallas_call(front_kernel, grid=(width // blk,), in_specs=[smem, smem,...  7.7 us
    pallas_call x1, Pallas kernels, back_call(): pl.pallas_call(back_kernel, grid=(width // blk,), in_specs=[smem, smem, p...  6.11 us
    ppermute x1, starting transfers between devices, on_device(): before = lax.ppermute(tokens[rows - EDGE:], AXES, up)  3.03 us
  transfers between devices with their start and end apart: 4, of which 3 were waited for; matrix products, arithmetic and copies ran while one was open for 1% of the time, Pallas kernels for 0%

commit v1 on v0

--- a/solution.py
+++ b/solution.py
@@ -15,7 +15,7 @@
 AXES = ("ctx", "head")
 LANES = 128
 EDGE = 16
-PER_STEP = 2
+PER_STEP = 4
 VMEM_ALL = 60 * 1024 * 1024
 VMEM_MOST = 44 * 1024 * 1024
 VMEM_SOME = 24 * 1024 * 1024
@@ -38,6 +38,10 @@
         start = jnp.where(past, end, start)
         stop = jnp.where(past, stop, jnp.minimum(stop, end))
     return start, stop
+
+
+def device_index():
+    return lax.axis_index("ctx") * lax.axis_size("head") + lax.axis_index("head")
 
 
 def low_lanes(shape):
@@ -76,7 +80,7 @@
 
 
 def front_kernel(
-    lengths_ref, where_ref, before_ref, x_ref, after_ref, taps_ref, w_ref, cot_ref, wo_ref,
+    lengths_ref, before_ref, x_ref, after_ref, taps_ref, w_ref, cot_ref, wo_ref,
     out_ref, padded, projected, d_rows,
 ):
     rows, blk = x_ref.shape
@@ -86,7 +90,7 @@
     padded[pl.ds(8, rows), :] = x_ref[...].astype(F32)
     padded[pl.ds(8 + rows, 8), :] = after_ref[...].astype(F32)[:8]
     mixed = conv_rows(
-        padded, range(blk // LANES), taps_ref, lengths_ref, where_ref[0], rows, False
+        padded, range(blk // LANES), taps_ref, lengths_ref, device_index() * rows, rows, False
     ).astype(BF16)
     d_rows[step] = lax.dot_general(
         cot_ref[...], wo_ref[...], (((1,), (1,)), ((), ())), preferred_element_type=F32
@@ -112,7 +116,7 @@
             out_ref[2 * pair + 1] = jnp.concatenate([zip_high(k, v), zip_high(q, d)]).astype(BF16)
 
 
-def front_call(lengths, where, before, x, after, taps, w_qkv, cotangent, w_out):
+def front_call(lengths, before, x, after, taps, w_qkv, cotangent, w_out):
     rows, width = x.shape
     heads = width // HD
     blk = 256
@@ -122,7 +126,7 @@
         front_kernel,
         grid=(width // blk,),
         in_specs=[
-            smem, smem, columns(before), columns(x), columns(after), columns(taps),
+            smem, columns(before), columns(x), columns(after), columns(taps),
             pl.BlockSpec((blk, 3 * width), lambda i: (i, 0)),
             pl.BlockSpec((rows, width), lambda i: (0, 0)),
             pl.BlockSpec((blk, width), lambda i: (i, 0)),
@@ -139,11 +143,11 @@
             flops=8 * rows * width * width, bytes_accessed=8 * width * width, transcendentals=0
         ),
         name="front",
-    )(lengths, where, before, x, after, taps, w_qkv, cotangent, w_out)
+    )(lengths, before, x, after, taps, w_qkv, cotangent, w_out)
 
 
 def attention_kernel(
-    pre, place, lengths_ref, where_ref, kv_mine, kv_other, qd_ref,
+    pre, place, lengths_ref, kv_mine, kv_other, qd_ref,
     cq_ref, dkv_mine, edge_mine, send_ref,
     visit_q, visit_k, keys_ref, turned_ref, qd_cat_ref, d_turned_ref, span_ref, e_ref,
     total_ref, context_ref, row_ref, d_query_ref, acc_ref, cq_full,
@@ -152,7 +156,9 @@
     key_slots, rows, _ = kv_mine.shape
     tile = 2 * rows
     tiles, groups = key_slots // 2, slots // 2
-    base, parity = where_ref[1], where_ref[2]
+    me = device_index()
+    window = 2 * slots
+    base, parity = me // window * (window * rows), me % 2
     origin = base - pre * tile
     unit = HD**-0.5
     to_exp2 = unit * math.log2(math.e)
@@ -178,8 +184,9 @@
             return count + 1
 
         count = lax.fori_loop(t_first, u + pre // 2 + 1, note, count)
-    visit_q[count] = groups
-    visit_k[count] = tiles
+    for i in range(PER_STEP - 1):
+        visit_q[count + i] = groups
+        visit_k[count + i] = tiles
 
     for t in range(tiles):
         for half, source in enumerate((kv_mine, kv_other)):
@@ -195,11 +202,12 @@
     for u in range(groups):
         qd = jnp.concatenate(
             [qd_ref[place(2 * u + i, 0), pl.ds(rows, rows)] for i in range(2)]
-        ).astype(F32)
+        )
+        d_turned_ref[u] = qd.T[HD:].astype(F32)
+        qd = qd.astype(F32)
         low = low_lanes(qd.shape)
         qd_cat_ref[u, pl.ds(0, tile)] = jnp.where(low, qd, 0.0).astype(BF16)
         qd_cat_ref[u, pl.ds(tile, tile)] = jnp.where(low, 0.0, qd).astype(BF16)
-        d_turned_ref[u] = qd.T[HD:]
         q_pos = base + u * (2 * tile) + parity * rows + lane_pos
         q_start, _ = record_span(q_pos, lengths_ref)
         span_ref[u, pl.ds(0, 1)] = q_start
@@ -293,7 +301,7 @@
         send_ref[pre + s, pl.ds(rows, 16)] = jnp.concatenate([d_edge, q_edge]).astype(BF16)
 
 
-def attention_call(lengths, where, kv_mine, kv_other, qd, pre):
+def attention_call(lengths, kv_mine, kv_other, qd, pre):
     slots = qd.shape[0]
     key_slots, rows, _ = kv_mine.shape
     tile = 2 * rows
@@ -305,7 +313,7 @@
     vmem = pl.BlockSpec(memory_space=pltpu.VMEM)
     return pl.pallas_call(
         functools.partial(attention_kernel, pre, place),
-        in_specs=[smem, smem, vmem, vmem, vmem],
+        in_specs=[smem, vmem, vmem, vmem],
         out_specs=[vmem, vmem, vmem, vmem],
         out_shape=[
             jax.ShapeDtypeStruct((slots, rows, LANES), BF16),
@@ -314,8 +322,8 @@
             jax.ShapeDtypeStruct((key_slots, rows + 16, LANES), BF16),
         ],
         scratch_shapes=[
-            pltpu.SMEM((visits + 1,), jnp.int32),
-            pltpu.SMEM((visits + 1,), jnp.int32),
+            pltpu.SMEM((visits,), jnp.int32),
+            pltpu.SMEM((visits,), jnp.int32),
             pltpu.VMEM((tiles + 1, 2 * tile, LANES), BF16),
             pltpu.VMEM((tiles + 1, LANES, 2 * tile), BF16),
             pltpu.VMEM((groups + 1, 2 * tile, LANES), BF16),
@@ -336,7 +344,7 @@
             transcendentals=slots * rows * MAXLEN,
         ),
         name="attention",
-    )(lengths, where, kv_mine, kv_other, qd)
+    )(lengths, kv_mine, kv_other, qd)
 
 
 def combine_kernel(cq_ref, mine_ref, edge_ref, got_ref, out_ref):
@@ -387,7 +395,7 @@
 
 
 def back_kernel(
-    lengths_ref, where_ref, r_ref, taps_ref, w_ref, wo_ref,
+    lengths_ref, r_ref, taps_ref, w_ref, wo_ref,
     attended_ref, grad_ref, context, grads, padded,
 ):
     heads = r_ref.shape[0]
@@ -425,11 +433,11 @@
     padded[pl.ds(8, rows), :] = mixed[:rows]
     padded[pl.ds(8 + rows, 8), :] = edge
     grad_ref[...] = conv_rows(
-        padded, range(blk // LANES), taps_ref, lengths_ref, where_ref[0], rows, True
+        padded, range(blk // LANES), taps_ref, lengths_ref, device_index() * rows, rows, True
     ).astype(BF16)
 
 
-def back_call(lengths, where, r, taps, w_qkv, w_out):
+def back_call(lengths, r, taps, w_qkv, w_out):
     heads = r.shape[0]
     rows = (r.shape[1] - 16) // 2
     width = heads * HD
@@ -441,7 +449,7 @@
         back_kernel,
         grid=(width // blk,),
         in_specs=[
-            smem, smem,
+            smem,
             pl.BlockSpec(r.shape, lambda i: (0, 0, 0)),
             pl.BlockSpec((KS, blk), lambda i: (0, i)),
             pl.BlockSpec((blk, 3 * width), lambda i: (i, 0)),
@@ -459,7 +467,7 @@
             flops=8 * rows * width * width, bytes_accessed=8 * width * width, transcendentals=0
         ),
         name="back",
-    )(lengths, where, r, taps, w_qkv, w_out)
+    )(lengths, r, taps, w_qkv, w_out)
 
 
 def bit_reversed(i, count):
@@ -477,7 +485,6 @@
     windows = devices // window
     pre = MAXLEN // (2 * rows) if windows > 1 else 0
     me = lax.axis_index(AXES)
-    where = jnp.stack([me * rows, me // window * (window * rows), me % 2]).astype(jnp.int32)
     same_side = [
         [w * window + 2 * bit_reversed(c, heads) + side for c in range(heads)]
         for w in range(windows)
@@ -494,7 +501,7 @@
 
     before = lax.ppermute(tokens[rows - EDGE :], AXES, up)
     after = lax.ppermute(tokens[:EDGE], AXES, down)
-    sent = front_call(lengths, where, before, tokens, after, conv_kernel, w_qkv, cotangent, w_out)
+    sent = front_call(lengths, before, tokens, after, conv_kernel, w_qkv, cotangent, w_out)
     qd = exchange(sent)
     kv_mine = qd[:, :rows]
     if pre:
@@ -502,13 +509,13 @@
         kv_mine = jnp.stack([kv_mine[bit_reversed(s, heads)] for s in range(heads)])
         kv_mine = jnp.concatenate([lax.ppermute(kv_mine[heads - pre :], AXES, shift), kv_mine])
     kv_other = lax.ppermute(kv_mine, AXES, swapped)
-    cq, mine, edge, send = attention_call(lengths, where, kv_mine, kv_other, qd, pre)
+    cq, mine, edge, send = attention_call(lengths, kv_mine, kv_other, qd, pre)
     got = lax.ppermute(send, AXES, swapped)
     if pre:
         grads = combine_windows(cq, mine, got, pre, me % 2, window, devices)
     else:
         grads = combine_call(cq, mine, edge, got)
-    return back_call(lengths, where, exchange(grads), conv_kernel, w_qkv, w_out)
+    return back_call(lengths, exchange(grads), conv_kernel, w_qkv, w_out)
 
 
 def solution(mesh):

time: 113 us -> 114 us (level)
  transfers between devices with their start and end apart: 4 -> 4, of which waited for: 3 -> 3; matrix products, arithmetic and copies ran while one was open for 1% -> 0% of each run, Pallas kernels for 0% -> 0%
where the time goes in v1:
time: 114 us
  blocking collectives  69.3 us (61%)
  Pallas kernels  33.2 us (29%)
  waiting for transfers between devices  4.59 us (4%)
  starting transfers between devices  4.58 us (4%)
  local copies, waits for them, and re-layouts  1.47 us (1%)
    all_to_all x2, blocking collectives, exchange(): lax.all_to_all(x, AXES, split_axis=0, concat_axis=0, axis_index_groups=sa...  69.3 us
    pallas_call x1, Pallas kernels, attention_call(): pl.pallas_call(functools.partial(attention_kernel, pre, place), in_specs=...  19.2 us
    pallas_call x1, Pallas kernels, front_call(): pl.pallas_call(front_kernel, grid=(width // blk,), in_specs=[smem, column...  7.74 us
    pallas_call x1, Pallas kernels, back_call(): pl.pallas_call(back_kernel, grid=(width // blk,), in_specs=[smem, pl.Bloc...  6.12 us
    ppermute x1, starting transfers between devices, on_device(): before = lax.ppermute(tokens[rows - EDGE:], AXES, up)  3.03 us
  transfers between devices with their start and end apart: 4, of which 3 were waited for; matrix products, arithmetic and copies ran while one was open for 0% of the time, Pallas kernels for 0%

profile of v1, /device:TPU:0, one launch (start us, length us, event | category | flops | bytes accessed | tf_op | source)
XLA Modules:
  0.0 113.9 jit_solution(10858834045509934342)
XLA Ops:
  0.6 0.8 fusion
  1.4 1.3 %collective-permute-start.1 = (bf16[16,1024]{1,0:T(8,128)(2,1)S(1)}, bf16[16,1024]{1,0:T(8,128)(2,1)S(1)}, u32[]{:S(2)}, u32[]{:S(2)}) collective-permute-start(bf16[16,1024]{1,0:T(8,128)(2,1)S(1)} %get-tuple-element.10), channel_id=1, source_target_pairs={{1,0},{2,1},{3,2},{4,3},{5,4},{6,5},{7,6},{8,7},{9,8},{10,9},{11,1... | collective-permute-start | bytes 98312 | tf_op jit(solution)/shard_map/ppermute | solution.py:503
  2.7 3.0 %collective-permute-start = (bf16[16,1024]{1,0:T(8,128)(2,1)S(1)}, bf16[16,1024]{1,0:T(8,128)(2,1)S(1)}, u32[]{:S(2)}, u32[]{:S(2)}) collective-permute-start(bf16[16,1024]{1,0:T(8,128)(2,1)S(1)} %get-tuple-element.11), channel_id=1, source_target_pairs={{0,1},{1,2},{2,3},{3,4},{4,5},{5,6},{6,7},{7,8},{8,9},{9,10},{10,1... | collective-permute-start | bytes 98312 | tf_op jit(solution)/shard_map/ppermute | solution.py:502
  5.7 0.0 collective-permute-done.1.after_ref
  5.7 0.0 copy-start.3
  5.8 0.8 collective-permute-done.before_ref
  6.6 0.0 copy-done.3
  6.6 0.6 copy-done.4
  7.2 7.7 %front.1 = bf16[16,256,128]{2,1,0:T(8,128)(2,1)} custom-call(s32[4]{0:T(128)} %lengths_ref.5, bf16[16,1024]{1,0:T(8,128)(2,1)} %copy-done.4, bf16[128,1024]{1,0:T(8,128)(2,1)} %x_ref.1, bf16[16,1024]{1,0:T(8,128)(2,1)} %copy-done.3, f32[7,1024]{1,0:T(8,128)} %taps_ref.3, bf16[1024,3072]{1,0:T(8,128)(2,1)} %w_ref.3, bf16[128,1024]{1,0:T(8,128)(2,1)} %cot_ref.1, ...), custom_call_target="tpu_custom_call" | custom-call | flops 1073741824 | bytes 8388608 | tf_op jit(solution)/shard_map/front/pallas_call | solution.py:125
  14.9 36.5 %all_to_all.10.qd_ref = bf16[16,256,128]{2,1,0:T(8,128)(2,1)S(1)} all-to-all(bf16[16,256,128]{2,1,0:T(8,128)(2,1)} %front.1), channel_id=1, replica_groups={{0,16,8,24,4,20,12,28,2,18,10,26,6,22,14,30},{1,17,9,25,5,21,13,29,3,19..., dimensions={0} | all-to-all | bytes 2097152 | tf_op jit(solution)/shard_map/all_to_all | solution.py:498
  51.4 0.0 slice-start.1
  51.5 0.1 collective-permute-start.2
  51.5 1.9 %collective-permute-done.2.kv_other = bf16[16,128,128]{2,1,0:T(8,128)(2,1)S(1)} collective-permute-done((bf16[16,128,128]{2,1,0:T(8,128)(2,1)S(1)}, bf16[16,128,128]{2,1,0:T(8,128)(2,1)S(1)}, u32[]{:S(2)}, u32[]{:S(2)}) %collective-permute-start.2) | collective-permute-done | bytes 524320 | tf_op jit(solution)/shard_map/ppermute | solution.py:511
  53.4 0.0 copy-done.2
  53.4 19.2 %attention.1 = (bf16[16,128,128]{2,1,0:T(8,128)(2,1)S(1)}, f32[16,128,128]{2,1,0:T(8,128)S(1)}, f32[16,8,128]{2,1,0:T(8,128)S(1)}, bf16[16,144,128]{2,1,0:T(8,128)(2,1)S(1)}) custom-call(s32[4]{0:T(128)S(1)} %copy-done.2, bf16[16,128,128]{2,1,0:T(8,128)(2,1)S(1)} %slice.12.kv_mine, bf16[16,128,128]{2,1,0:T(8,128)(2,1)S(1)} %collective-permute-done.2.kv_other, ...), custom_call_target="tpu_custom_call" | custom-call | flops 5368709120 | bytes 5242880 | tf_op jit(solution)/shard_map/attention/pallas_call | solution.py:314
  72.6 0.2 collective-permute-start.3
  72.8 1.9 %collective-permute-done.3.got_ref = bf16[16,144,128]{2,1,0:T(8,128)(2,1)S(1)} collective-permute-done((bf16[16,144,128]{2,1,0:T(8,128)(2,1)S(1)}, bf16[16,144,128]{2,1,0:T(8,128)(2,1)S(1)}, u32[]{:S(2)}, u32[]{:S(2)}) %collective-permute-start.3) | collective-permute-done | bytes 589856 | tf_op jit(solution)/shard_map/ppermute | solution.py:513
  74.7 0.2 combine.1
  74.8 32.9 %all_to_all.11.r_ref = bf16[16,272,128]{2,1,0:T(8,128)(2,1)S(1)} all-to-all(bf16[16,272,128]{2,1,0:T(8,128)(2,1)S(1)} %combine.1), channel_id=1, replica_groups={{0,16,8,24,4,20,12,28,2,18,10,26,6,22,14,30},{1,17,9,25,5,21,13,29,3,19..., dimensions={0} | all-to-all | bytes 2228224 | tf_op jit(solution)/shard_map/all_to_all | solution.py:498
  107.7 0.0 slice-done
  107.7 0.0 slice-done.1
  107.7 0.0 copy-done
  107.7 0.0 copy-done.1
  107.8 6.1 %back.1 = (bf16[128,1024]{1,0:T(8,128)(2,1)}, bf16[128,1024]{1,0:T(8,128)(2,1)}) custom-call(s32[4]{0:T(128)S(1)} %copy-done.2, bf16[16,272,128]{2,1,0:T(8,128)(2,1)S(1)} %all_to_all.11.r_ref, f32[7,1024]{1,0:T(8,128)S(1)} %copy-done.1, bf16[1024,3072]{1,0:T(8,128)(2,1)S(1)} %bitcast.1, bf16[1024,1024]{1,0:T(8,128)(2,1)S(1)} %copy-done), custom_call_target="tpu_custom_call" | custom-call | flops 1073741824 | bytes 8388608 | tf_op jit(solution)/shard_map/back/pallas_call | solution.py:448
  (7 shorter events, 0.0 us)
Async XLA Ops:
  1.4 4.3 %collective-permute-start.1 = (bf16[16,1024]{1,0:T(8,128)(2,1)S(1)}, bf16[16,1024]{1,0:T(8,128)(2,1)S(1)}, u32[]{:S(2)}, u32[]{:S(2)}) collective-permute-start(bf16[16,1024]{1,0:T(8,128)(2,1)S(1)} %get-tuple-element.10), channel_id=1, source_target_pairs={{1,0},{2,1},{3,2},{4,3},{5,4},{6,5},{7,6},{8,7},{9,8},{10,9},{11,1... | collective-permute-start | bytes 98312 | tf_op jit(solution)/shard_map/ppermute | solution.py:503
  2.7 3.9 %collective-permute-start = (bf16[16,1024]{1,0:T(8,128)(2,1)S(1)}, bf16[16,1024]{1,0:T(8,128)(2,1)S(1)}, u32[]{:S(2)}, u32[]{:S(2)}) collective-permute-start(bf16[16,1024]{1,0:T(8,128)(2,1)S(1)} %get-tuple-element.11), channel_id=1, source_target_pairs={{0,1},{1,2},{2,3},{3,4},{4,5},{5,6},{6,7},{7,8},{8,9},{9,10},{10,1... | collective-permute-start | bytes 98312 | tf_op jit(solution)/shard_map/ppermute | solution.py:502
  5.7 0.8 copy-start.3
  6.6 0.6 copy-start.4
  14.9 38.5 %copy-start.2 = (s32[4]{0:T(128)S(1)}, s32[4]{0:T(128)}, u32[]{:S(2)}) copy-start(s32[4]{0:T(128)} %lengths_ref.5) | copy-start | bytes 52
  51.4 56.3 %slice-start = ((s8[6291456]{0:T(1024)(128)(4,1)}), s8[4194304]{0:T(1024)(128)(4,1)S(1)}, s32[]{:S(2)}) async-start(s8[6291456]{0:T(1024)(128)(4,1)} %bitcast), calls=%async_computation.2 | async-start | bytes 8388608
  51.4 56.3 %slice-start.1 = ((s8[6291456]{0:T(1024)(128)(4,1)}), s8[2097152]{0:T(1024)(128)(4,1)S(1)}, s32[]{:S(2)}) async-start(s8[6291456]{0:T(1024)(128)(4,1)} %bitcast), calls=%async_computation.3 | async-start | bytes 4194304
  51.5 2.0 %collective-permute-start.2 = (bf16[16,128,128]{2,1,0:T(8,128)(2,1)S(1)}, bf16[16,128,128]{2,1,0:T(8,128)(2,1)S(1)}, u32[]{:S(2)}, u32[]{:S(2)}) collective-permute-start(bf16[16,128,128]{2,1,0:T(8,128)(2,1)S(1)} %slice.12.kv_mine), channel_id=1, source_target_pairs={{0,1},{1,0},{2,3},{3,2},{4,5},{5,4},{6,7},{7,6},{8,9},{9,8},{10,11... | collective-permute-start | bytes 1572872 | tf_op jit(solution)/shard_map/ppermute | solution.py:511
  72.6 2.1 %collective-permute-start.3 = (bf16[16,144,128]{2,1,0:T(8,128)(2,1)S(1)}, bf16[16,144,128]{2,1,0:T(8,128)(2,1)S(1)}, u32[]{:S(2)}, u32[]{:S(2)}) collective-permute-start(bf16[16,144,128]{2,1,0:T(8,128)(2,1)S(1)} %get-tuple-element.9), channel_id=1, source_target_pairs={{0,1},{1,0},{2,3},{3,2},{4,5},{5,4},{6,7},{7,6},{8,9},{9,8},{10,11... | collective-permute-start | bytes 1769480 | tf_op jit(solution)/shard_map/ppermute | solution.py:513
  74.7 33.1 %copy-start = (bf16[1024,1024]{1,0:T(8,128)(2,1)S(1)}, bf16[1024,1024]{1,0:T(8,128)(2,1)}, u32[]{:S(2)}) copy-start(bf16[1024,1024]{1,0:T(8,128)(2,1)} %wo_ref.3) | copy-start | bytes 6291460
  74.7 33.1 %copy-start.1 = (f32[7,1024]{1,0:T(8,128)S(1)}, f32[7,1024]{1,0:T(8,128)}, u32[]{:S(2)}) copy-start(f32[7,1024]{1,0:T(8,128)} %taps_ref.3) | copy-start | bytes 86020
